TPU v7x, 128 devices: a whole 4x4x4 slice. The times are simulated.
128 devices in a mesh: row: 8 (over x_lo, z), col: 16 (over y, x_hi, core).
Axes of the slice: x: 4 (x_hi: 2, x_lo: 2; x = x_hi * 2 + x_lo), y: 4, z: 4, core: 2. Of those that a mesh axis runs over, the one named last changes fastest.
Arguments:
- features: bfloat16 [128, 32768], P('col', 'row'), may hold values from -6 to 6
- weight: bfloat16 [128, 256], P('col'), may hold values from -0.5 to 0.5
- cotangent: bfloat16 [256, 32768], P('col', 'row'), may hold values from -6 to 6
- adjacency: bfloat16 [5120, 128, 128], P('row')
- tile_rows: int32 [5120], P('row'), may hold values from 0 to 31
- tile_cols: int32 [5120], P('row'), may hold values from 0 to 255, as said below
- tile_count: int32 [8], P('row'), may hold values from 160 to 640, as said below
- node_count: int32 [8], P('row'), may hold values from 2048 to 4096, as said below
Outputs:
- hidden_out: bfloat16 [256, 32768], P('col', 'row')
- grad_weight: float32 [128, 256], P('col')
- grad_features: bfloat16 [128, 32768], P('col', 'row')
Inputs may be any that keep to these rules, and one draw needn't show every extreme that they name: tile_count[b] is the number of used slots of row block b, the first ones of its 640 slots; some row block uses all 640. `tile_cols`: over the used slots of one row block the column tiles never fall. node_count[b] real nodes lead row block b, the rest are padding; some row block is full.
All inputs are finite; a program needn't handle non-finite values.
Results may differ from a plain program's by a relative error of at most 0.0049.
Values may be sent and summed in bfloat16 or wider, within the bound.
A program may use at most 128 MiB of HBM per device.

v0:
```python
import jax
import jax.numpy as jnp
from jax import lax
from jax.sharding import PartitionSpec as P

TILE = 128


def slot_bounds(tile_cols, in_use, first_tile, last_tile):
    low_slot = jnp.sum((in_use & (tile_cols < first_tile)).astype(jnp.int32))
    high_slot = jnp.sum((in_use & (tile_cols < last_tile)).astype(jnp.int32))
    return (low_slot, high_slot)


def over_groups(adjacency, tile_rows, tile_cols, low_slot, high_slot, update, initial):
    slot_total = adjacency.shape[0]
    group_size = min(32, slot_total)
    rounds = (high_slot - low_slot + group_size - 1) // group_size

    def one_round(number, running):
        opening = low_slot + number * group_size
        anchor = jnp.minimum(opening, slot_total - group_size)
        within = anchor + lax.iota(jnp.int32, group_size)
        chosen = (within >= opening) & (within < jnp.minimum(high_slot, opening + group_size))
        block_tiles = lax.dynamic_slice_in_dim(adjacency, anchor, group_size, 0)
        block_rows = lax.dynamic_slice_in_dim(tile_rows, anchor, group_size, 0)
        block_cols = lax.dynamic_slice_in_dim(tile_cols, anchor, group_size, 0)
        return update(running, block_tiles, block_rows, block_cols, chosen)

    return lax.fori_loop(0, rounds, one_round, initial)


def local(features, weight, cotangent, adjacency, tile_rows, tile_cols, tile_count, node_count):
    feature_rows, nodes_dev = features.shape
    row_tiles = nodes_dev // TILE
    slot_total = adjacency.shape[0]
    living = lax.iota(jnp.int32, nodes_dev) < node_count[0]
    in_use = lax.iota(jnp.int32, slot_total) < tile_count[0]
    masked = jnp.where(living[None, :], features, jnp.zeros_like(features))
    zero_sums = jnp.zeros((feature_rows, row_tiles, TILE), jnp.float32)
    portion = lax.all_gather(masked, "row", axis=1, tiled=True)
    first_tile = jnp.int32(0) // TILE
    width_tiles = portion.shape[1] // TILE
    low_slot, high_slot = slot_bounds(tile_cols, in_use, first_tile, first_tile + width_tiles)
    blocks = portion.reshape(feature_rows, width_tiles, TILE)

    def update(totals, block_tiles, block_rows, block_cols, chosen):
        local_cols = jnp.clip(block_cols, 0, width_tiles - 1)
        sources = jnp.take(blocks, local_cols, axis=1)
        products = jnp.einsum(
            "fgm,gnm->gfn", sources, block_tiles, preferred_element_type=jnp.float32
        )
        placing = (
            (block_rows[:, None] == lax.iota(jnp.int32, row_tiles)[None, :]) & chosen[:, None]
        ).astype(jnp.float32)
        return totals + jnp.einsum(
            "gi,gfn->fin", placing, products, precision=lax.Precision.HIGHEST
        )

    summed = over_groups(adjacency, tile_rows, tile_cols, low_slot, high_slot, update, zero_sums)
    aggregate = jnp.where(living[None, :], summed.reshape(feature_rows, nodes_dev), 0.0).astype(
        jnp.bfloat16
    )
    columns = weight
    hidden_sum = lax.psum_scatter(
        jnp.einsum("fh,fn->hn", columns, aggregate, preferred_element_type=jnp.float32),
        "col",
        scatter_dimension=0,
        tiled=True,
    )
    hidden_out = hidden_sum.astype(jnp.bfloat16)
    portion = lax.all_gather(cotangent, "col", axis=0, tiled=True)
    grad_block = jnp.einsum("fn,hn->fh", aggregate, portion, preferred_element_type=jnp.float32)
    columns = weight
    back_part = jnp.einsum("fh,hn->fn", columns, portion, preferred_element_type=jnp.float32)
    total_nodes = nodes_dev * lax.axis_size("row")
    grad_weight = lax.psum(grad_block, "row") * float(total_nodes) ** (-0.5)
    back_rows = jnp.where(living[None, :], back_part, 0.0).astype(jnp.bfloat16)
    back_blocks = back_rows.reshape(feature_rows, row_tiles, TILE)
    offset = jnp.int32(0)
    low_slot, high_slot = slot_bounds(
        tile_cols, in_use, offset, offset + row_tiles * lax.axis_size("row")
    )

    def update(totals, block_tiles, block_rows, block_cols, chosen):
        sources = jnp.take(back_blocks, jnp.clip(block_rows, 0, row_tiles - 1), axis=1)
        products = jnp.einsum(
            "fgn,gnm->gfm", sources, block_tiles, preferred_element_type=jnp.float32
        )
        placing = (
            (block_cols[:, None] == lax.iota(jnp.int32, row_tiles * lax.axis_size("row"))[None, :])
            & chosen[:, None]
        ).astype(jnp.float32)
        return totals + jnp.einsum(
            "gj,gfm->jfm", placing, products, precision=lax.Precision.HIGHEST
        )

    column_parts = lax.psum_scatter(
        over_groups(
            adjacency,
            tile_rows,
            tile_cols,
            low_slot,
            high_slot,
            update,
            jnp.zeros((row_tiles * lax.axis_size("row"), feature_rows, TILE), jnp.float32),
        ),
        "row",
        scatter_dimension=0,
        tiled=True,
    )
    grad_sum = jnp.transpose(column_parts, (1, 0, 2)).reshape(feature_rows, nodes_dev)
    grad_features = jnp.where(living[None, :], grad_sum, 0.0).astype(jnp.bfloat16)
    return (hidden_out, grad_weight, grad_features)


def solution(mesh):
    placed = (
        P("col", "row"),
        P("col", None),
        P("col", "row"),
        P("row", None, None),
        P("row"),
        P("row"),
        P("row"),
        P("row"),
    )
    return jax.shard_map(
        local,
        mesh=mesh,
        in_specs=placed,
        out_specs=(P("col", "row"), P("col", None), P("col", "row")),
        check_vma=False,
    )
```

profile of v0, /device:TPU:1, one launch (start us, length us, event | category | flops | bytes accessed | tf_op | source)
XLA Modules:
  0.0 458.1 jit_solution(14837763405731346772)
XLA Ops:
  8.6 1.4 convert_reduce_fusion
  12.0 49.6 %all-gather.2.cloned.1.call-done = bf16[256,4096]{1,0:T(8,128)(2,1)} async-done(((bf16[16,4096]{1,0:T(8,128)(2,1)}), bf16[256,4096]{1,0:T(8,128)(2,1)}) %all-gather.2.cloned.1.call-update) | async-done | bytes 2097168 | tf_op jit(solution)/shard_map/all_gather | solution.py:72
  61.6 2.0 fusion.30
  63.7 42.4 %while.21 = (s32[]{:T(128)}, f32[256,8,128]{2,0,1:T(8,128)S(1)}, s32[]{:T(128)}, s32[]{:T(128)}, s32[640]{0:T(1024)}, /*index=5*/s32[]{:T(128)}, s32[640]{0:T(10...) while((s32[]{:T(128)}, f32[256,8,128]{2,0,1:T(8,128)S(1)}, ...), condition=%wide.region_7.8_spmd, body=%wide.region_6.7_spmd.sunk | while | flops 109364584 | bytes 3609851 | solution.py:30
  65.8 0.8 compare_and_fusion.10
  67.2 1.7 fusion.65
  68.8 0.9 convolution_add_fusion.2
  71.9 0.8 compare_and_fusion.10
  73.2 1.7 fusion.65
  74.9 0.9 convolution_add_fusion.2
  77.9 0.8 compare_and_fusion.10
  79.3 1.7 fusion.65
  80.9 0.9 convolution_add_fusion.2
  84.0 0.8 compare_and_fusion.10
  85.3 1.7 fusion.65
  87.0 0.9 convolution_add_fusion.2
  90.0 0.8 compare_and_fusion.10
  91.4 1.7 fusion.65
  93.0 0.9 convolution_add_fusion.2
  96.1 0.8 compare_and_fusion.10
  97.4 1.7 fusion.65
  99.1 0.9 convolution_add_fusion.2
  102.1 0.8 compare_and_fusion.10
  103.5 1.7 fusion.65
  105.2 0.9 convolution_add_fusion.2
  106.1 1.0 copy-done.1
  107.1 109.4 %reduce-scatter.5.cloned.1.call-done = f32[32,8,128]{2,0,1:T(8,128)} async-done(((f32[256,8,128]{2,0,1:T(8,128)}), f32[32,8,128]{2,0,1:T(8,128)}) %reduce-scatter.5.cloned.1.call-update) | async-done | bytes 131088 | tf_op jit(solution)/shard_map/reduce_scatter | solution.py:98
  216.5 1.6 fusion.31
  218.1 22.5 %all_gather.6 = bf16[8,32768]{1,0:T(8,128)(2,1)S(1)} all-gather(bf16[8,4096]{1,0:T(8,128)(2,1)S(1)} %get-tuple-element.171), channel_id=1, replica_groups=mesh['row'=8,'col'=16] {'row'}, dimensions={1}, use_global_device_ids=true | all-gather | bytes 589824 | tf_op jit(solution)/shard_map/all_gather | solution.py:41
  240.6 39.6 %while.20 = (s32[]{:T(128)}, f32[8,32,128]{2,1,0:T(8,128)S(1)}, s32[]{:T(128)}, s32[]{:T(128)}, s32[640]{0:T(1024)}, /*index=5*/bf16[8,256,128]{2,0,1:T(8,128)(2...) while((s32[]{:T(128)}, f32[8,32,128]{2,1,0:T(8,128)S(1)}, ...), condition=%wide.region_3.4_spmd, body=%wide.region_2.3_spmd.sunk | while | flops 21040488 | bytes 1774843 | solution.py:30
  242.7 0.8 compare_and_fusion.8
  244.1 1.9 fusion.59
  248.4 0.8 compare_and_fusion.8
  249.7 1.9 fusion.59
  254.0 0.8 compare_and_fusion.8
  255.4 1.9 fusion.59
  261.1 1.9 fusion.59
  265.4 0.8 compare_and_fusion.8
  266.7 1.9 fusion.59
  272.4 1.9 fusion.59
  278.0 1.9 fusion.59
  280.2 2.7 convolution_bitcast_fusion.1
  282.9 5.6 %copy.18 = f32[256,4096]{1,0:T(8,128)} copy(f32[256,4096]{0,1:T(8,128)} %convolution_bitcast_fusion.1) | data formatting | bytes 8388608
  288.6 1.6 copy-done.2
  290.8 86.4 %psum.7 = f32[8,256]{1,0:T(8,128)S(1)} all-reduce(f32[8,256]{1,0:T(8,128)S(1)} %fusion.33), channel_id=1, replica_groups=mesh['row'=8,'col'=16] {'row'}, use_global_device_ids=true, to_apply=%region_5.6 | all-reduce | flops 2048 | bytes 16384 | tf_op jit(solution)/shard_map/psum | solution.py:77
  377.8 71.3 %reduce-scatter.7.cloned.1.call-done = f32[16,4096]{1,0:T(8,128)} async-done(((f32[256,4096]{1,0:T(8,128)}), f32[16,4096]{1,0:T(8,128)}) %reduce-scatter.7.cloned.1.call-update) | async-done | bytes 262160
  449.1 1.4 copy.19
  450.6 1.0 copy.17
  (83 shorter events, 25.4 us)
Async XLA Ops:
  7.2 54.4 %copy-start = (bf16[8,256]{1,0:T(8,128)(2,1)S(1)}, bf16[8,256]{1,0:T(8,128)(2,1)}, u32[]{:S(2)}) copy-start(bf16[8,256]{1,0:T(8,128)(2,1)} %param.13) | copy-start | bytes 12292
  7.2 54.4 %all-gather.2.cloned.1.call-start = ((), (), s32[]{:S(2)}) async-start(), calls=%async_computation.2 | async-start | bytes 2228224 | tf_op jit(solution)/shard_map/all_gather | solution.py:72
  7.9 208.6 %reduce-scatter.5.cloned.1.call-start = ((), (), s32[]{:S(2)}) async-start(), calls=%async_computation.3 | async-start | bytes 1179648 | tf_op jit(solution)/shard_map/reduce_scatter | solution.py:98
  63.6 152.8 %copy-start.3 = (bf16[8,4096]{1,0:T(8,128)(2,1)S(1)}, bf16[8,4096]{1,0:T(8,128)(2,1)}, u32[]{:S(2)}) copy-start(bf16[8,4096]{1,0:T(8,128)(2,1)} %param.12) | copy-start | bytes 196612
  106.0 1.0 copy-start.1
  107.0 342.1 %reduce-scatter.7.cloned.1.call-start = ((), (), s32[]{:S(2)}) async-start(), calls=%async_computation.4 | async-start | bytes 4456448
  288.6 1.6 copy-start.2
Sparse Core Ops, SparseCore 0:
  10.5 51.0 all-gather.1
  107.2 109.2 reduce-scatter.4
  288.7 160.3 reduce-scatter.6
where the time goes:
time: 464 us; the launch traced here: 458 us
  waiting for transfers between devices  231 us (50%)
  blocking collectives  109 us (23%)
  matrix products  38.1 us (8%)
  local copies, waits for them, and re-layouts  29.7 us (6%)
  loops' own time  19.3 us (4%)
  between operations  16.5 us (4%)
  other arithmetic  14.6 us (3%)
    reduce_scatter x1, waiting for transfers between devices, local(): lax.psum_scatter(over_groups(adjacency, tile_rows, tile_cols, low_slot, h...  109 us
    psum x1, blocking collectives, local(): grad_weight = lax.psum(grad_block, 'row') * float(total_nodes) ** (-0.5)  86.4 us
    unnamed x4, waiting for transfers between devices  72 us
    all_gather x1, waiting for transfers between devices, local(): portion = lax.all_gather(cotangent, 'col', axis=0, tiled=True)  49.6 us
    all_gather x1, blocking collectives, local(): portion = lax.all_gather(masked, 'row', axis=1, tiled=True)  22.5 us
    another operation x2, loops' own time, over_groups(): return lax.fori_loop(0, rounds, one_round, initial)  19.3 us
    dot_general x7, matrix products, update(): jnp.einsum('fgm,gnm->gfn', sources, block_tiles, preferred_element_type=j...  13.3 us
    dot_general x7, matrix products, update(): jnp.einsum('fgn,gnm->gfm', sources, block_tiles, preferred_element_type=j...  11.6 us
  transfers between devices with their start and end apart: 3, of which 3 were waited for; matrix products, arithmetic and copies ran while one was open for 1% of the time, Pallas kernels for 0%

commit v1 on v0

v1 whole, which is shorter than its diff:
```python
import functools

import jax
import jax.numpy as jnp
from jax import lax
from jax.experimental import pallas as pl
from jax.experimental.pallas import tpu as pltpu
from jax.sharding import PartitionSpec as P

TILE = 128
MESH = pl.DeviceIdType.MESH
NT = (((1,), (1,)), ((), ()))
NN = (((1,), (0,)), ((), ()))
BF = jnp.bfloat16
F32 = jnp.float32


def kernel(
    rows, cols, slots, chunks, unroll,
    feat_ref, weight_ref, cot_ref, adj_hbm, trow_s, tcol_s, trow_v, tcol_v, tcount, ncount,
    hid_ref, gw_ref, gf_ref,
    adj, fstage, fgath, cgath, wstage, wgath, bstage, bgath, prod, sums, gstage, ggath,
    astage, agath, hstage, wpart, wpgath, wrow, wrgath, chosen_c, chosen_r,
    adj_sem, own_sem, send_sem, recv_sem,
):
    me_r = lax.axis_index("row")
    me_c = lax.axis_index("col")
    tiles_dev = 2 * cols
    node_total = rows * tiles_dev * TILE
    per_chunk = slots // chunks

    def adj_copy(i):
        part = pl.ds(i * per_chunk, per_chunk)
        return pltpu.make_async_copy(adj_hbm.at[part], adj.at[part], adj_sem.at[i])

    for i in range(chunks):
        adj_copy(i).start()

    barrier = pltpu.get_barrier_semaphore()

    def greet_row(k, carry):
        pl.semaphore_signal(barrier, inc=1, device_id=(lax.rem(me_r + k, rows), me_c), device_id_type=MESH)
        return carry

    def greet_col(k, carry):
        pl.semaphore_signal(barrier, inc=1, device_id=(me_r, lax.rem(me_c + k, cols)), device_id_type=MESH)
        return carry

    lax.fori_loop(1, rows, greet_row, 0)
    lax.fori_loop(1, cols, greet_col, 0)

    live_count = ncount[0]
    used = tcount[0]

    lane = lax.broadcasted_iota(jnp.int32, (8, TILE), 1)
    for p in range(cols):
        halves = []
        for h in range(2):
            at = (2 * p + h) * TILE
            block = feat_ref[:, at:at + TILE].astype(F32)
            halves.append(jnp.where(lane + at < live_count, block, 0.0))
        fstage[p] = jnp.concatenate(halves, axis=0).astype(BF)
    wstage[...] = weight_ref[...].astype(F32)

    pl.semaphore_wait(barrier, rows + cols - 2)

    def to_col(phase, source, target):
        def one(k, carry):
            peer = lax.rem(me_c + k, cols)
            pltpu.make_async_remote_copy(
                src_ref=source(peer), dst_ref=target, send_sem=send_sem.at[phase], recv_sem=recv_sem.at[phase],
                device_id=(me_r, peer), device_id_type=MESH,
            ).start()
            return carry

        lax.fori_loop(1, cols, one, 0)

    def to_row(phase, source, target):
        def one(k, carry):
            peer = lax.rem(me_r + k, rows)
            pltpu.make_async_remote_copy(
                src_ref=source(peer), dst_ref=target, send_sem=send_sem.at[phase], recv_sem=recv_sem.at[phase],
                device_id=(peer, me_c), device_id_type=MESH,
            ).start()
            return carry

        lax.fori_loop(1, rows, one, 0)

    def arrived(phase, ref):
        pltpu.make_async_copy(ref, ref, recv_sem.at[phase]).wait()

    def sent(phase, ref):
        pltpu.make_async_copy(ref, ref, send_sem.at[phase]).wait()

    def slice_cols(index):
        return pl.ds(pl.multiple_of(index * 2 * TILE, 2 * TILE), 2 * TILE)

    to_col(0, lambda d: cot_ref.at[:, slice_cols(d)], cgath.at[me_c])
    to_col(1, lambda d: wstage, wgath.at[me_c])
    to_row(2, lambda d: fstage, fgath.at[me_r])
    own_c = pltpu.make_async_copy(cot_ref.at[:, slice_cols(me_c)], cgath.at[me_c], own_sem.at[0])
    own_w = pltpu.make_async_copy(wstage, wgath.at[me_c], own_sem.at[1])
    own_f = pltpu.make_async_copy(fstage, fgath.at[me_r], own_sem.at[2])
    own_c.start()
    own_w.start()
    own_f.start()

    slot_used = lax.broadcasted_iota(jnp.int32, (1, slots), 1) < used
    key_c = jnp.where(slot_used, tcol_v[...], -1)
    key_r = jnp.where(slot_used, trow_v[...], -1)
    chosen_c[...] = (
        lax.broadcasted_iota(jnp.int32, (rows * tiles_dev, slots), 0) == key_c
    ).astype(F32).astype(BF)
    chosen_r[...] = (lax.broadcasted_iota(jnp.int32, (tiles_dev, slots), 0) == key_r).astype(F32).astype(BF)

    own_c.wait()
    own_w.wait()
    arrived(0, cgath.at[pl.ds(0, cols - 1)])
    arrived(1, wgath.at[pl.ds(0, cols - 1)])
    whole_w = wgath[...].reshape(cols * 8, -1).astype(BF)
    cot_nodes = cgath[...].reshape(cols * 16, 2 * TILE)
    back = lax.dot_general(whole_w, cot_nodes, NN, preferred_element_type=F32)
    node = lax.broadcasted_iota(jnp.int32, back.shape, 1) + me_c * (2 * TILE)
    back = jnp.where(node < live_count, back, 0.0)
    for d in range(cols):
        part = back[8 * d:8 * d + 8]
        bstage[d] = jnp.concatenate([part[:, :TILE], part[:, TILE:]], axis=0).astype(BF)
    to_col(3, lambda d: bstage.at[d], bgath.at[me_c])
    own_b = pltpu.make_async_copy(bstage.at[me_c], bgath.at[me_c], own_sem.at[3])
    own_b.start()
    own_b.wait()
    arrived(3, bgath.at[pl.ds(0, cols - 1)])

    zero = jnp.zeros((16, TILE), BF)

    def tile_pass(source, index_s, forward):
        group = 4 * unroll

        def step(g, carry):
            for u in range(unroll):
                s = pl.multiple_of(g * group, group) + 4 * u
                at = [index_s[s + i] for i in range(4)]
                x = [source[at[i] // 2] for i in range(4)]
                spread = (
                    [[x[0], zero], [x[1], zero], [zero, x[2]], [zero, x[3]]]
                    if forward
                    else [[x[0], zero], [zero, x[1]], [x[2], zero], [zero, x[3]]]
                )
                left = jnp.concatenate([jnp.concatenate(pair, axis=1) for pair in spread], axis=0)
                right = jnp.concatenate(
                    [adj[pl.ds(s, 2)].reshape(2 * TILE, TILE), adj[pl.ds(s + 2, 2)].reshape(2 * TILE, TILE)], axis=1
                )
                out = lax.dot_general(left, right, NT if forward else NN, preferred_element_type=F32)
                for i in range(4):
                    half = i % 2 if forward else i // 2
                    block = out[16 * i:16 * i + 16, TILE * half:TILE * half + TILE]
                    block = jnp.where(at[i] % 2 == 0, block[:8], block[8:])
                    block = jnp.where(s + i < used, block, 0.0)
                    prod[pl.ds(pl.multiple_of((s + i) * 8, 8), 8), :] = block
            return carry

        return step

    def add_up(chosen, tiles):
        picks = chosen[...]
        for f in range(0, 8, 2):
            pair = jnp.concatenate([prod[pl.ds(f + j, slots, stride=8), :] for j in range(2)], axis=1)
            high = pair.astype(BF)
            low = (pair - high.astype(F32)).astype(BF)
            total = lax.dot_general(picks, high, NN, preferred_element_type=F32) + lax.dot_general(
                picks, low, NN, preferred_element_type=F32
            )
            for j in range(2):
                sums[pl.ds(f + j, tiles, stride=8), :] = total[:, TILE * j:TILE * j + TILE]

    groups = slots // (4 * unroll)
    per_group = chunks // groups if chunks > groups else 1

    def backward_step(g, carry):
        adj_copy(g).wait()
        return tile_pass(bgath, trow_s, False)(g, carry)

    lax.fori_loop(0, groups, backward_step, 0)
    add_up(chosen_c, rows * tiles_dev)
    for d in range(rows):
        size = tiles_dev * 8
        gstage[d] = sums[d * size:(d + 1) * size, :].reshape(cols, 16, TILE).astype(BF)
    to_row(4, lambda d: gstage.at[d], ggath.at[me_r])
    own_g = pltpu.make_async_copy(gstage.at[me_r], ggath.at[me_r], own_sem.at[4])
    own_g.start()

    own_f.wait()
    arrived(2, fgath.at[pl.ds(0, rows - 1)])
    features = fgath.reshape(rows * cols, 16, TILE)
    lax.fori_loop(0, groups, tile_pass(features, tcol_s, True), 0)
    add_up(chosen_r, tiles_dev)
    for d in range(cols):
        halves = []
        for h in range(2):
            at = 2 * d + h
            block = sums[8 * at:8 * at + 8, :]
            halves.append(jnp.where(lane + at * TILE < live_count, block, 0.0))
        astage[d] = jnp.concatenate(halves, axis=0).astype(BF)
    to_col(5, lambda d: astage.at[d], agath.at[me_c])
    own_a = pltpu.make_async_copy(astage.at[me_c], agath.at[me_c], own_sem.at[5])
    own_a.start()
    own_a.wait()
    arrived(5, agath.at[pl.ds(0, cols - 1)])

    spread = agath[...].astype(F32)
    agg = jnp.concatenate(
        [spread[:, :8].reshape(cols * 8, TILE), spread[:, 8:].reshape(cols * 8, TILE)], axis=1
    ).astype(BF)
    gw = lax.dot_general(agg, cgath[...].reshape(cols * 16, 2 * TILE), NT, preferred_element_type=F32)
    wpart[...] = gw.reshape(cols, 8, gw.shape[1])
    to_col(6, lambda d: wpart.at[d], wpgath.at[me_c])
    whole_w = wgath[...].reshape(cols * 8, -1).astype(BF)
    hidden = lax.dot_general(whole_w, agg, (((0,), (0,)), ((), ())), preferred_element_type=F32)
    hstage[...] = hidden.astype(BF).reshape(cols, 16, 2 * TILE)
    to_col(7, lambda d: hstage.at[d], hid_ref.at[:, slice_cols(me_c)])
    own_h = pltpu.make_async_copy(hstage.at[me_c], hid_ref.at[:, slice_cols(me_c)], own_sem.at[6])
    own_h.start()
    own_p = pltpu.make_async_copy(wpart.at[me_c], wpgath.at[me_c], own_sem.at[7])
    own_p.start()

    own_g.wait()
    arrived(4, ggath.at[pl.ds(0, rows - 1)])
    for p in range(cols):
        total = ggath[0, p].astype(F32)
        for d in range(1, rows):
            total = total + ggath[d, p].astype(F32)
        for h in range(2):
            at = (2 * p + h) * TILE
            gf_ref[:, at:at + TILE] = jnp.where(lane + at < live_count, total[8 * h:8 * h + 8], 0.0).astype(BF)

    own_p.wait()
    arrived(6, wpgath.at[pl.ds(0, cols - 1)])
    wrow[...] = jnp.sum(wpgath[...], axis=0)
    to_row(8, lambda d: wrow, wrgath.at[me_r])
    own_r = pltpu.make_async_copy(wrow, wrgath.at[me_r], own_sem.at[8])
    own_r.start()
    own_r.wait()
    arrived(8, wrgath.at[pl.ds(0, rows - 1)])
    total = wrgath[0]
    for d in range(1, rows):
        total = total + wrgath[d]
    gw_ref[...] = total * float(node_total) ** (-0.5)

    own_h.wait()
    arrived(7, hstage.at[pl.ds(0, cols - 1)])
    sent(0, cgath.at[pl.ds(0, cols - 1)])
    sent(1, wgath.at[pl.ds(0, cols - 1)])
    sent(2, fgath.at[pl.ds(0, rows - 1)])
    sent(3, bgath.at[pl.ds(0, cols - 1)])
    sent(4, ggath.at[pl.ds(0, rows - 1)])
    sent(5, agath.at[pl.ds(0, cols - 1)])
    sent(6, wpgath.at[pl.ds(0, cols - 1)])
    sent(7, hstage.at[pl.ds(0, cols - 1)])
    sent(8, wrgath.at[pl.ds(0, rows - 1)])


def solution(mesh):
    rows, cols = mesh.shape["row"], mesh.shape["col"]

    def local(features, weight, cotangent, adjacency, tile_rows, tile_cols, tile_count, node_count):
        slots = adjacency.shape[0]
        feats, nodes = features.shape
        hid = weight.shape[1]
        tiles = nodes // TILE
        unroll = 20
        groups = slots // (4 * unroll)
        smem = pl.BlockSpec(memory_space=pltpu.SMEM)
        vmem = pl.BlockSpec(memory_space=pltpu.VMEM)
        return pl.pallas_call(
            functools.partial(kernel, rows, cols, slots, groups, unroll),
            out_shape=(
                jax.ShapeDtypeStruct(cotangent.shape, BF),
                jax.ShapeDtypeStruct(weight.shape, F32),
                jax.ShapeDtypeStruct(features.shape, BF),
            ),
            in_specs=[vmem, vmem, vmem, pl.BlockSpec(memory_space=pl.ANY), smem, smem, vmem, vmem, smem, smem],
            out_specs=(vmem, vmem, vmem),
            scratch_shapes=[
                pltpu.VMEM((slots, TILE, TILE), BF),
                pltpu.VMEM((cols, 16, TILE), BF),
                pltpu.VMEM((rows, cols, 16, TILE), BF),
                pltpu.VMEM((cols, 16, 2 * TILE), BF),
                pltpu.VMEM((8, hid), F32),
                pltpu.VMEM((cols, 8, hid), F32),
                pltpu.VMEM((cols, 16, TILE), BF),
                pltpu.VMEM((cols, 16, TILE), BF),
                pltpu.VMEM((slots * 8, TILE), F32),
                pltpu.VMEM((rows * tiles * 8, TILE), F32),
                pltpu.VMEM((rows, cols, 16, TILE), BF),
                pltpu.VMEM((rows, cols, 16, TILE), BF),
                pltpu.VMEM((cols, 16, TILE), BF),
                pltpu.VMEM((cols, 16, TILE), BF),
                pltpu.VMEM((cols, 16, 2 * TILE), BF),
                pltpu.VMEM((cols, 8, hid), F32),
                pltpu.VMEM((cols, 8, hid), F32),
                pltpu.VMEM((8, hid), F32),
                pltpu.VMEM((rows, 8, hid), F32),
                pltpu.VMEM((rows * tiles, slots), BF),
                pltpu.VMEM((tiles, slots), BF),
                pltpu.SemaphoreType.DMA((groups,)),
                pltpu.SemaphoreType.DMA((9,)),
                pltpu.SemaphoreType.DMA((9,)),
                pltpu.SemaphoreType.DMA((9,)),
            ],
            compiler_params=pltpu.CompilerParams(
                collective_id=0, has_side_effects=True, vmem_limit_bytes=60 * 2**20
            ),
        )(
            features, weight, cotangent, adjacency, tile_rows, tile_cols,
            tile_rows.reshape(1, slots), tile_cols.reshape(1, slots), tile_count, node_count,
        )

    return jax.shard_map(
        local,
        mesh=mesh,
        in_specs=(
            P("col", "row"), P("col", None), P("col", "row"), P("row", None, None),
            P("row"), P("row"), P("row"), P("row"),
        ),
        out_specs=(P("col", "row"), P("col", None), P("col", "row")),
        check_vma=False,
    )
```

time: 464 us -> 60.9 us (0.13); the launches traced: 458 us -> 60.6 us
  waiting for transfers between devices: 231 us -> 0 us
  blocking collectives: 109 us -> 0 us
  Pallas kernels: 0 us -> 51.8 us
  matrix products: 38.1 us -> 0 us
  local copies, waits for them, and re-layouts: 29.7 us -> 6.87 us
  loops' own time: 19.3 us -> 0 us
  other arithmetic: 14.6 us -> 0 us
  between operations: 16.5 us -> 1.93 us
    reduce_scatter x1 -> x0, waiting for transfers between devices: 109 us -> none  [local(): lax.psum_scatter(over_groups(adjacency, tile_rows, tile_cols, low_slot, h...]
    psum x1 -> x0, blocking collectives: 86.4 us -> none  [local(): grad_weight = lax.psum(grad_block, 'row') * float(total_nodes) ** (-0.5)]
    unnamed x4 -> x0, waiting for transfers between devices: 72 us -> none
    pallas_call x0 -> x1, Pallas kernels: none -> 51.8 us  [local(): pl.pallas_call(functools.partial(kernel, rows, cols, slots, groups, unrol...]
    all_gather x1 -> x0, waiting for transfers between devices: 49.6 us -> none  [local(): portion = lax.all_gather(cotangent, 'col', axis=0, tiled=True)]
    dot_general x31 -> x0, matrix products: 38.1 us -> none  [the longest x7 13.3 us: update(): jnp.einsum('fgm,gnm->gfn', sources, block_tiles, preferred_element_type=j...]
    all_gather x1 -> x0, blocking collectives: 22.5 us -> none  [local(): portion = lax.all_gather(masked, 'row', axis=1, tiled=True)]
    another operation x2 -> x0, loops' own time: 19.3 us -> none  [over_groups(): return lax.fori_loop(0, rounds, one_round, initial)]
  transfers between devices with their start and end apart: 3 -> 0, of which waited for: 3 -> 0; matrix products, arithmetic and copies ran while one was open for 1% -> 0% of each run, Pallas kernels for 0% -> 0%
where the time goes in v1:
time: 60.9 us; the launch traced here: 60.6 us
  Pallas kernels  51.8 us (85%)
  local copies, waits for them, and re-layouts  6.87 us (11%)
  between operations  1.93 us (3%)
    pallas_call x1, Pallas kernels, local(): pl.pallas_call(functools.partial(kernel, rows, cols, slots, groups, unrol...  51.8 us
    unnamed x3, local copies, waits for them, and re-layouts  4.34 us
    reshape x1, local copies, waits for them, and re-layouts, local(): tile_rows.reshape(1, slots)  1.27 us
    reshape x1, local copies, waits for them, and re-layouts, local(): tile_cols.reshape(1, slots)  1.27 us

profile of v1, /device:TPU:1, one launch (start us, length us, event | category | flops | bytes accessed | tf_op | source)
XLA Modules:
  0.0 60.6 jit_solution(3642813541936917082)
XLA Ops:
  1.9 1.3 %reshape.12.trow_v = s32[1,640]{1,0:T(1,128)} reshape(s32[640]{0:T(1024)} %trow_s.1) | data formatting | bytes 5120 | tf_op jit(solution)/shard_map/reshape | solution.py:315
  3.2 1.3 %reshape.13.tcol_v = s32[1,640]{1,0:T(1,128)} reshape(s32[640]{0:T(1024)} %tcol_s.1) | data formatting | bytes 5120 | tf_op jit(solution)/shard_map/reshape | solution.py:315
  4.5 51.8 %shard_map.103 = (bf16[16,4096]{1,0:T(8,128)(2,1)}, f32[8,256]{1,0:T(8,128)}, bf16[8,4096]{1,0:T(8,128)(2,1)}) custom-call(bf16[8,4096]{1,0:T(8,128)(2,1)} %feat_ref.1, bf16[8,256]{1,0:T(8,128)(2,1)} %weight_ref.1, bf16[16,4096]{1,0:T(8,128)(2,1)} %cot_ref.1, bf16[640,128,128]{2,1,0:T(8,128)(2,1)} %adj_hbm.1, s32[640]{0:T(1024)} %trow_s.1, s32[640]{0:T(1024)} %tcol_s.1, ...), custom_call_target="tpu_custom_call" | custom-call | tf_op jit(solution)/shard_map/pallas_call | solution.py:274
  56.2 1.6 %copy.16 = bf16[16,4096]{1,0:T(8,128)(2,1)} copy(bf16[16,4096]{1,0:T(8,128)(2,1)} %get-tuple-element.6) | data formatting | bytes 262144
  57.8 1.3 %copy.17 = f32[8,256]{1,0:T(8,128)} copy(f32[8,256]{1,0:T(8,128)} %get-tuple-element.7) | data formatting | bytes 16384
  59.1 1.5 %copy.18 = bf16[8,4096]{1,0:T(8,128)(2,1)} copy(bf16[8,4096]{1,0:T(8,128)(2,1)} %get-tuple-element.8) | data formatting | bytes 131072

commit v2 on v1

--- a/solution.py
+++ b/solution.py
@@ -17,11 +17,11 @@
 
 def kernel(
     rows, cols, slots, chunks, unroll,
-    feat_ref, weight_ref, cot_ref, adj_hbm, trow_s, tcol_s, trow_v, tcol_v, tcount, ncount,
+    feat_hbm, weight_hbm, cot_hbm, adj_hbm, trow_s, tcol_s, trow_v, tcol_v, tcount, ncount,
     hid_ref, gw_ref, gf_ref,
-    adj, fstage, fgath, cgath, wstage, wgath, bstage, bgath, prod, sums, gstage, ggath,
+    feat_ref, weight_ref, cot_ref, adj, fstage, fgath, cgath, wstage, wgath, bstage, bgath, prod, sums, gstage, ggath,
     astage, agath, hstage, wpart, wpgath, wrow, wrgath, chosen_c, chosen_r,
-    adj_sem, own_sem, send_sem, recv_sem,
+    adj_sem, in_sem, own_sem, send_sem, recv_sem,
 ):
     me_r = lax.axis_index("row")
     me_c = lax.axis_index("col")
@@ -33,8 +33,6 @@
         part = pl.ds(i * per_chunk, per_chunk)
         return pltpu.make_async_copy(adj_hbm.at[part], adj.at[part], adj_sem.at[i])
 
-    for i in range(chunks):
-        adj_copy(i).start()
 
     barrier = pltpu.get_barrier_semaphore()
 
@@ -49,10 +47,22 @@
     lax.fori_loop(1, rows, greet_row, 0)
     lax.fori_loop(1, cols, greet_col, 0)
 
+    inputs = [
+        pltpu.make_async_copy(feat_hbm, feat_ref, in_sem.at[0]),
+        pltpu.make_async_copy(cot_hbm, cot_ref, in_sem.at[1]),
+        pltpu.make_async_copy(weight_hbm, weight_ref, in_sem.at[2]),
+    ]
+    for copy in inputs:
+        copy.start()
+    for i in range(chunks):
+        adj_copy(i).start()
+
     live_count = ncount[0]
     used = tcount[0]
 
     lane = lax.broadcasted_iota(jnp.int32, (8, TILE), 1)
+    for copy in inputs:
+        copy.wait()
     for p in range(cols):
         halves = []
         for h in range(2):
@@ -106,8 +116,8 @@
     own_f.start()
 
     slot_used = lax.broadcasted_iota(jnp.int32, (1, slots), 1) < used
-    key_c = jnp.where(slot_used, tcol_v[...], -1)
-    key_r = jnp.where(slot_used, trow_v[...], -1)
+    key_c = jnp.where(slot_used, tcol_v[...].reshape(1, slots), -1)
+    key_r = jnp.where(slot_used, trow_v[...].reshape(1, slots), -1)
     chosen_c[...] = (
         lax.broadcasted_iota(jnp.int32, (rows * tiles_dev, slots), 0) == key_c
     ).astype(F32).astype(BF)
@@ -128,9 +138,6 @@
     to_col(3, lambda d: bstage.at[d], bgath.at[me_c])
     own_b = pltpu.make_async_copy(bstage.at[me_c], bgath.at[me_c], own_sem.at[3])
     own_b.start()
-    own_b.wait()
-    arrived(3, bgath.at[pl.ds(0, cols - 1)])
-
     zero = jnp.zeros((16, TILE), BF)
 
     def tile_pass(source, index_s, forward):
@@ -173,26 +180,17 @@
             for j in range(2):
                 sums[pl.ds(f + j, tiles, stride=8), :] = total[:, TILE * j:TILE * j + TILE]
 
-    groups = slots // (4 * unroll)
-    per_group = chunks // groups if chunks > groups else 1
-
-    def backward_step(g, carry):
-        adj_copy(g).wait()
-        return tile_pass(bgath, trow_s, False)(g, carry)
-
-    lax.fori_loop(0, groups, backward_step, 0)
-    add_up(chosen_c, rows * tiles_dev)
-    for d in range(rows):
-        size = tiles_dev * 8
-        gstage[d] = sums[d * size:(d + 1) * size, :].reshape(cols, 16, TILE).astype(BF)
-    to_row(4, lambda d: gstage.at[d], ggath.at[me_r])
-    own_g = pltpu.make_async_copy(gstage.at[me_r], ggath.at[me_r], own_sem.at[4])
-    own_g.start()
-
     own_f.wait()
     arrived(2, fgath.at[pl.ds(0, rows - 1)])
     features = fgath.reshape(rows * cols, 16, TILE)
-    lax.fori_loop(0, groups, tile_pass(features, tcol_s, True), 0)
+    groups = slots // (4 * unroll)
+    forward = tile_pass(features, tcol_s, True)
+
+    def forward_step(g, carry):
+        adj_copy(g).wait()
+        return forward(g, carry)
+
+    lax.fori_loop(0, groups, forward_step, 0)
     add_up(chosen_r, tiles_dev)
     for d in range(cols):
         halves = []
@@ -204,6 +202,11 @@
     to_col(5, lambda d: astage.at[d], agath.at[me_c])
     own_a = pltpu.make_async_copy(astage.at[me_c], agath.at[me_c], own_sem.at[5])
     own_a.start()
+    own_b.wait()
+    arrived(3, bgath.at[pl.ds(0, cols - 1)])
+
+    backward = tile_pass(bgath, trow_s, False)
+    lax.fori_loop(0, groups - 1, backward, 0)
     own_a.wait()
     arrived(5, agath.at[pl.ds(0, cols - 1)])
 
@@ -223,6 +226,21 @@
     own_p = pltpu.make_async_copy(wpart.at[me_c], wpgath.at[me_c], own_sem.at[7])
     own_p.start()
 
+    lax.fori_loop(groups - 1, groups, backward, 0)
+    add_up(chosen_c, rows * tiles_dev)
+    for d in range(rows):
+        size = tiles_dev * 8
+        gstage[d] = sums[d * size:(d + 1) * size, :].reshape(cols, 16, TILE).astype(BF)
+    to_row(4, lambda d: gstage.at[d], ggath.at[me_r])
+    own_g = pltpu.make_async_copy(gstage.at[me_r], ggath.at[me_r], own_sem.at[4])
+    own_g.start()
+
+    own_p.wait()
+    arrived(6, wpgath.at[pl.ds(0, cols - 1)])
+    wrow[...] = jnp.sum(wpgath[...], axis=0)
+    to_row(8, lambda d: wrow, wrgath.at[me_r])
+    own_r = pltpu.make_async_copy(wrow, wrgath.at[me_r], own_sem.at[8])
+    own_r.start()
     own_g.wait()
     arrived(4, ggath.at[pl.ds(0, rows - 1)])
     for p in range(cols):
@@ -233,12 +251,6 @@
             at = (2 * p + h) * TILE
             gf_ref[:, at:at + TILE] = jnp.where(lane + at < live_count, total[8 * h:8 * h + 8], 0.0).astype(BF)
 
-    own_p.wait()
-    arrived(6, wpgath.at[pl.ds(0, cols - 1)])
-    wrow[...] = jnp.sum(wpgath[...], axis=0)
-    to_row(8, lambda d: wrow, wrgath.at[me_r])
-    own_r = pltpu.make_async_copy(wrow, wrgath.at[me_r], own_sem.at[8])
-    own_r.start()
     own_r.wait()
     arrived(8, wrgath.at[pl.ds(0, rows - 1)])
     total = wrgath[0]
@@ -259,6 +271,18 @@
     sent(8, wrgath.at[pl.ds(0, rows - 1)])
 
 
+def finish(a_in, b_in, c_in, a_out, b_out, c_out, sems):
+    copies = [
+        pltpu.make_async_copy(a_in, a_out, sems.at[0]),
+        pltpu.make_async_copy(b_in, b_out, sems.at[1]),
+        pltpu.make_async_copy(c_in, c_out, sems.at[2]),
+    ]
+    for copy in copies:
+        copy.start()
+    for copy in copies:
+        copy.wait()
+
+
 def solution(mesh):
     rows, cols = mesh.shape["row"], mesh.shape["col"]
 
@@ -271,16 +295,20 @@
         groups = slots // (4 * unroll)
         smem = pl.BlockSpec(memory_space=pltpu.SMEM)
         vmem = pl.BlockSpec(memory_space=pltpu.VMEM)
-        return pl.pallas_call(
+        anywhere = pl.BlockSpec(memory_space=pl.ANY)
+        partial_out = pl.pallas_call(
             functools.partial(kernel, rows, cols, slots, groups, unroll),
             out_shape=(
                 jax.ShapeDtypeStruct(cotangent.shape, BF),
                 jax.ShapeDtypeStruct(weight.shape, F32),
                 jax.ShapeDtypeStruct(features.shape, BF),
             ),
-            in_specs=[vmem, vmem, vmem, pl.BlockSpec(memory_space=pl.ANY), smem, smem, vmem, vmem, smem, smem],
+            in_specs=[anywhere] * 4 + [smem, smem, vmem, vmem, smem, smem],
             out_specs=(vmem, vmem, vmem),
             scratch_shapes=[
+                pltpu.VMEM(features.shape, BF),
+                pltpu.VMEM(weight.shape, BF),
+                pltpu.VMEM(cotangent.shape, BF),
                 pltpu.VMEM((slots, TILE, TILE), BF),
                 pltpu.VMEM((cols, 16, TILE), BF),
                 pltpu.VMEM((rows, cols, 16, TILE), BF),
@@ -303,6 +331,7 @@
                 pltpu.VMEM((rows * tiles, slots), BF),
                 pltpu.VMEM((tiles, slots), BF),
                 pltpu.SemaphoreType.DMA((groups,)),
+                pltpu.SemaphoreType.DMA((3,)),
                 pltpu.SemaphoreType.DMA((9,)),
                 pltpu.SemaphoreType.DMA((9,)),
                 pltpu.SemaphoreType.DMA((9,)),
@@ -312,8 +341,15 @@
             ),
         )(
             features, weight, cotangent, adjacency, tile_rows, tile_cols,
-            tile_rows.reshape(1, slots), tile_cols.reshape(1, slots), tile_count, node_count,
+            tile_rows, tile_cols, tile_count, node_count,
         )
+        return pl.pallas_call(
+            finish,
+            out_shape=[jax.ShapeDtypeStruct(x.shape, x.dtype) for x in partial_out],
+            in_specs=[anywhere] * 3,
+            out_specs=[anywhere] * 3,
+            scratch_shapes=[pltpu.SemaphoreType.DMA((3,))],
+        )(*partial_out)
 
     return jax.shard_map(
         local,

time: 60.9 us -> 58.8 us (0.966)
  local copies, waits for them, and re-layouts: 6.87 us -> 0 us
  Pallas kernels: 51.8 us -> 56.7 us
    pallas_call x0 -> x1, Pallas kernels: none -> 7.33 us  [local(): pl.pallas_call(finish, out_shape=[jax.ShapeDtypeStruct(x.shape, x.dtype)...]
    unnamed x3 -> x0, local copies, waits for them, and re-layouts: 4.34 us -> none
    reshape x2 -> x0, local copies, waits for them, and re-layouts: 2.53 us -> none  [the longest x1 1.27 us: local(): tile_rows.reshape(1, slots)]
    pallas_call x1, Pallas kernels: 51.8 us -> 49.4 us  [local(): pl.pallas_call(functools.partial(kernel, rows, cols, slots, groups, unrol...]
where the time goes in v2:
time: 58.8 us; the launch traced here: 58.6 us
  Pallas kernels  56.7 us (96%)
  between operations  1.93 us (3%)
    pallas_call x1, Pallas kernels, local(): pl.pallas_call(functools.partial(kernel, rows, cols, slots, groups, unrol...  49.4 us
    pallas_call x1, Pallas kernels, local(): pl.pallas_call(finish, out_shape=[jax.ShapeDtypeStruct(x.shape, x.dtype)...  7.33 us

profile of v2, /device:TPU:1, one launch (start us, length us, event | category | flops | bytes accessed | tf_op | source)
XLA Modules:
  0.0 58.6 jit_solution(11015548191023119015)
XLA Ops:
  1.9 49.4 %shard_map.103 = (bf16[16,4096]{1,0:T(8,128)(2,1)}, f32[8,256]{1,0:T(8,128)}, bf16[8,4096]{1,0:T(8,128)(2,1)}) custom-call(bf16[8,4096]{1,0:T(8,128)(2,1)} %feat_hbm.1, bf16[8,256]{1,0:T(8,128)(2,1)} %weight_hbm.1, bf16[16,4096]{1,0:T(8,128)(2,1)} %cot_hbm.1, bf16[640,128,128]{2,1,0:T(8,128)(2,1)} %adj_hbm.1, s32[640]{0:T(1024)} %trow_v.1, s32[640]{0:T(1024)} %tcol_v.1, ...), custom_call_target="tpu_custom_call" | custom-call | tf_op jit(solution)/shard_map/pallas_call | solution.py:299
  51.3 7.3 %shard_map.104 = (bf16[16,4096]{1,0:T(8,128)(2,1)}, f32[8,256]{1,0:T(8,128)}, bf16[8,4096]{1,0:T(8,128)(2,1)}) custom-call(bf16[16,4096]{1,0:T(8,128)(2,1)} %get-tuple-element.6.a_in, f32[8,256]{1,0:T(8,128)} %get-tuple-element.7.b_in, bf16[8,4096]{1,0:T(8,128)(2,1)} %get-tuple-element.8.c_in), custom_call_target="tpu_custom_call" | custom-call | tf_op jit(solution)/shard_map/pallas_call | solution.py:346

commit v3 on v2

--- a/solution.py
+++ b/solution.py
@@ -54,7 +54,8 @@
     ]
     for copy in inputs:
         copy.start()
-    for i in range(chunks):
+    early = 2
+    for i in range(early):
         adj_copy(i).start()
 
     live_count = ncount[0]
@@ -70,7 +71,9 @@
             block = feat_ref[:, at:at + TILE].astype(F32)
             halves.append(jnp.where(lane + at < live_count, block, 0.0))
         fstage[p] = jnp.concatenate(halves, axis=0).astype(BF)
-    wstage[...] = weight_ref[...].astype(F32)
+    whalf = weight_ref.shape[1] // 2
+    w32 = weight_ref[...].astype(F32)
+    wstage[...] = jnp.concatenate([w32[:, :whalf], w32[:, whalf:]], axis=0).astype(BF)
 
     pl.semaphore_wait(barrier, rows + cols - 2)
 
@@ -102,12 +105,20 @@
     def sent(phase, ref):
         pltpu.make_async_copy(ref, ref, send_sem.at[phase]).wait()
 
+    def unstack(ref):
+        x = ref[...].astype(F32)
+        width = x.shape[2]
+        sides = [x[:, :8].reshape(-1, width), x[:, 8:].reshape(-1, width)]
+        return jnp.concatenate(sides, axis=1).astype(BF)
+
     def slice_cols(index):
         return pl.ds(pl.multiple_of(index * 2 * TILE, 2 * TILE), 2 * TILE)
 
     to_col(0, lambda d: cot_ref.at[:, slice_cols(d)], cgath.at[me_c])
     to_col(1, lambda d: wstage, wgath.at[me_c])
     to_row(2, lambda d: fstage, fgath.at[me_r])
+    for i in range(early, chunks):
+        adj_copy(i).start()
     own_c = pltpu.make_async_copy(cot_ref.at[:, slice_cols(me_c)], cgath.at[me_c], own_sem.at[0])
     own_w = pltpu.make_async_copy(wstage, wgath.at[me_c], own_sem.at[1])
     own_f = pltpu.make_async_copy(fstage, fgath.at[me_r], own_sem.at[2])
@@ -127,7 +138,7 @@
     own_w.wait()
     arrived(0, cgath.at[pl.ds(0, cols - 1)])
     arrived(1, wgath.at[pl.ds(0, cols - 1)])
-    whole_w = wgath[...].reshape(cols * 8, -1).astype(BF)
+    whole_w = unstack(wgath)
     cot_nodes = cgath[...].reshape(cols * 16, 2 * TILE)
     back = lax.dot_general(whole_w, cot_nodes, NN, preferred_element_type=F32)
     node = lax.broadcasted_iota(jnp.int32, back.shape, 1) + me_c * (2 * TILE)
@@ -210,14 +221,11 @@
     own_a.wait()
     arrived(5, agath.at[pl.ds(0, cols - 1)])
 
-    spread = agath[...].astype(F32)
-    agg = jnp.concatenate(
-        [spread[:, :8].reshape(cols * 8, TILE), spread[:, 8:].reshape(cols * 8, TILE)], axis=1
-    ).astype(BF)
+    agg = unstack(agath)
     gw = lax.dot_general(agg, cgath[...].reshape(cols * 16, 2 * TILE), NT, preferred_element_type=F32)
     wpart[...] = gw.reshape(cols, 8, gw.shape[1])
     to_col(6, lambda d: wpart.at[d], wpgath.at[me_c])
-    whole_w = wgath[...].reshape(cols * 8, -1).astype(BF)
+    whole_w = unstack(wgath)
     hidden = lax.dot_general(whole_w, agg, (((0,), (0,)), ((), ())), preferred_element_type=F32)
     hstage[...] = hidden.astype(BF).reshape(cols, 16, 2 * TILE)
     to_col(7, lambda d: hstage.at[d], hid_ref.at[:, slice_cols(me_c)])
@@ -271,16 +279,10 @@
     sent(8, wrgath.at[pl.ds(0, rows - 1)])
 
 
-def finish(a_in, b_in, c_in, a_out, b_out, c_out, sems):
-    copies = [
-        pltpu.make_async_copy(a_in, a_out, sems.at[0]),
-        pltpu.make_async_copy(b_in, b_out, sems.at[1]),
-        pltpu.make_async_copy(c_in, c_out, sems.at[2]),
-    ]
-    for copy in copies:
-        copy.start()
-    for copy in copies:
-        copy.wait()
+def finish(a_in, b_in, c_in, a_out, b_out, c_out):
+    a_out[...] = a_in[...]
+    b_out[...] = b_in[...]
+    c_out[...] = c_in[...]
 
 
 def solution(mesh):
@@ -313,8 +315,8 @@
                 pltpu.VMEM((cols, 16, TILE), BF),
                 pltpu.VMEM((rows, cols, 16, TILE), BF),
                 pltpu.VMEM((cols, 16, 2 * TILE), BF),
-                pltpu.VMEM((8, hid), F32),
-                pltpu.VMEM((cols, 8, hid), F32),
+                pltpu.VMEM((16, hid // 2), BF),
+                pltpu.VMEM((cols, 16, hid // 2), BF),
                 pltpu.VMEM((cols, 16, TILE), BF),
                 pltpu.VMEM((cols, 16, TILE), BF),
                 pltpu.VMEM((slots * 8, TILE), F32),
@@ -346,9 +348,8 @@
         return pl.pallas_call(
             finish,
             out_shape=[jax.ShapeDtypeStruct(x.shape, x.dtype) for x in partial_out],
-            in_specs=[anywhere] * 3,
-            out_specs=[anywhere] * 3,
-            scratch_shapes=[pltpu.SemaphoreType.DMA((3,))],
+            in_specs=[vmem] * 3,
+            out_specs=[vmem] * 3,
         )(*partial_out)
 
     return jax.shard_map(

time: 58.8 us -> 48.9 us (0.83)
  Pallas kernels: 56.7 us -> 46.7 us
    pallas_call x1, Pallas kernels: 7.33 us -> 1.61 us  [local(): pl.pallas_call(finish, out_shape=[jax.ShapeDtypeStruct(x.shape, x.dtype)...]
    pallas_call x1, Pallas kernels: 49.4 us -> 45.1 us  [local(): pl.pallas_call(functools.partial(kernel, rows, cols, slots, groups, unrol...]
where the time goes in v3:
time: 48.9 us; the launch traced here: 48.7 us
  Pallas kernels  46.7 us (96%)
  between operations  1.93 us (4%)
    pallas_call x1, Pallas kernels, local(): pl.pallas_call(functools.partial(kernel, rows, cols, slots, groups, unrol...  45.1 us
    pallas_call x1, Pallas kernels, local(): pl.pallas_call(finish, out_shape=[jax.ShapeDtypeStruct(x.shape, x.dtype)...  1.61 us

profile of v3, /device:TPU:1, one launch (start us, length us, event | category | flops | bytes accessed | tf_op | source)
XLA Modules:
  0.0 48.7 jit_solution(11712717281869668086)
XLA Ops:
  1.9 45.1 %shard_map.103 = (bf16[16,4096]{1,0:T(8,128)(2,1)}, f32[8,256]{1,0:T(8,128)}, bf16[8,4096]{1,0:T(8,128)(2,1)}) custom-call(bf16[8,4096]{1,0:T(8,128)(2,1)} %feat_hbm.1, bf16[8,256]{1,0:T(8,128)(2,1)} %weight_hbm.1, bf16[16,4096]{1,0:T(8,128)(2,1)} %cot_hbm.1, bf16[640,128,128]{2,1,0:T(8,128)(2,1)} %adj_hbm.1, s32[640]{0:T(1024)} %trow_v.1, s32[640]{0:T(1024)} %tcol_v.1, ...), custom_call_target="tpu_custom_call" | custom-call | tf_op jit(solution)/shard_map/pallas_call | solution.py:301
  47.1 1.6 %shard_map.104 = (bf16[16,4096]{1,0:T(8,128)(2,1)}, f32[8,256]{1,0:T(8,128)}, bf16[8,4096]{1,0:T(8,128)(2,1)}) custom-call(bf16[16,4096]{1,0:T(8,128)(2,1)} %get-tuple-element.6.a_in, f32[8,256]{1,0:T(8,128)} %get-tuple-element.7.b_in, bf16[8,4096]{1,0:T(8,128)(2,1)} %get-tuple-element.8.c_in), custom_call_target="tpu_custom_call" | custom-call | tf_op jit(solution)/shard_map/pallas_call | solution.py:348

commit v4 on v3

--- a/solution.py
+++ b/solution.py
@@ -19,21 +19,29 @@
     rows, cols, slots, chunks, unroll,
     feat_hbm, weight_hbm, cot_hbm, adj_hbm, trow_s, tcol_s, trow_v, tcol_v, tcount, ncount,
     hid_ref, gw_ref, gf_ref,
-    feat_ref, weight_ref, cot_ref, adj, fstage, fgath, cgath, wstage, wgath, bstage, bgath, prod, sums, gstage, ggath,
-    astage, agath, hstage, wpart, wpgath, wrow, wrgath, chosen_c, chosen_r,
-    adj_sem, in_sem, own_sem, send_sem, recv_sem,
+    feat_ref, weight_ref, cot_ref, adj, fstage, fgath, cgath, wstage, wgath, bstage, bgath, bsib, cline,
+    prod, pown, gsib, grecv, gstage, ggath, gsum,
+    astage, agath, apart, hstage, wpart, wfinal, chosen_c, chosen_r,
+    adj_sem, in_sem, own_sem, send_sem, recv_sem, pair_send, pair_recv, grad_sem,
 ):
     me_r = lax.axis_index("row")
     me_c = lax.axis_index("col")
+    core = lax.rem(me_c, 2)
+    sibling = me_c + 1 - 2 * core
+    line = me_c // 4
+    side_x = lax.rem(me_c // 2, 2)
+    partner = me_c + 2 - 4 * side_x
     tiles_dev = 2 * cols
-    node_total = rows * tiles_dev * TILE
+    tiles_all = rows * tiles_dev
+    node_total = tiles_all * TILE
+    half = slots // 2
+    base = core * half
     per_chunk = slots // chunks
 
     def adj_copy(i):
         part = pl.ds(i * per_chunk, per_chunk)
         return pltpu.make_async_copy(adj_hbm.at[part], adj.at[part], adj_sem.at[i])
 
-
     barrier = pltpu.get_barrier_semaphore()
 
     def greet_row(k, carry):
@@ -44,7 +52,12 @@
         pl.semaphore_signal(barrier, inc=1, device_id=(me_r, lax.rem(me_c + k, cols)), device_id_type=MESH)
         return carry
 
+    def greet_partner(k, carry):
+        pl.semaphore_signal(barrier, inc=1, device_id=(lax.rem(me_r + k, rows), partner), device_id_type=MESH)
+        return carry
+
     lax.fori_loop(1, rows, greet_row, 0)
+    lax.fori_loop(1, rows, greet_partner, 0)
     lax.fori_loop(1, cols, greet_col, 0)
 
     inputs = [
@@ -75,7 +88,7 @@
     w32 = weight_ref[...].astype(F32)
     wstage[...] = jnp.concatenate([w32[:, :whalf], w32[:, whalf:]], axis=0).astype(BF)
 
-    pl.semaphore_wait(barrier, rows + cols - 2)
+    pl.semaphore_wait(barrier, 2 * rows + cols - 3)
 
     def to_col(phase, source, target):
         def one(k, carry):
@@ -99,11 +112,23 @@
 
         lax.fori_loop(1, rows, one, 0)
 
+    def to_pair(phase, source, target):
+        pltpu.make_async_remote_copy(
+            src_ref=source, dst_ref=target, send_sem=pair_send.at[phase], recv_sem=pair_recv.at[phase],
+            device_id=(me_r, sibling), device_id_type=MESH,
+        ).start()
+
     def arrived(phase, ref):
         pltpu.make_async_copy(ref, ref, recv_sem.at[phase]).wait()
 
     def sent(phase, ref):
         pltpu.make_async_copy(ref, ref, send_sem.at[phase]).wait()
+
+    def pair_arrived(phase, ref):
+        pltpu.make_async_copy(ref, ref, pair_recv.at[phase]).wait()
+
+    def pair_sent(phase, ref):
+        pltpu.make_async_copy(ref, ref, pair_send.at[phase]).wait()
 
     def unstack(ref):
         x = ref[...].astype(F32)
@@ -117,6 +142,11 @@
     to_col(0, lambda d: cot_ref.at[:, slice_cols(d)], cgath.at[me_c])
     to_col(1, lambda d: wstage, wgath.at[me_c])
     to_row(2, lambda d: fstage, fgath.at[me_r])
+    for k in range(1, 4):
+        pltpu.make_async_remote_copy(
+            src_ref=cot_ref, dst_ref=cline.at[line, core], send_sem=send_sem.at[8], recv_sem=recv_sem.at[8],
+            device_id=(me_r, lax.rem(me_c + 4 * k, cols)), device_id_type=MESH,
+        ).start()
     for i in range(early, chunks):
         adj_copy(i).start()
     own_c = pltpu.make_async_copy(cot_ref.at[:, slice_cols(me_c)], cgath.at[me_c], own_sem.at[0])
@@ -125,13 +155,14 @@
     own_c.start()
     own_w.start()
     own_f.start()
-
-    slot_used = lax.broadcasted_iota(jnp.int32, (1, slots), 1) < used
-    key_c = jnp.where(slot_used, tcol_v[...].reshape(1, slots), -1)
-    key_r = jnp.where(slot_used, trow_v[...].reshape(1, slots), -1)
-    chosen_c[...] = (
-        lax.broadcasted_iota(jnp.int32, (rows * tiles_dev, slots), 0) == key_c
-    ).astype(F32).astype(BF)
+    own_l = pltpu.make_async_copy(cot_ref, cline.at[line, core], own_sem.at[4])
+    own_l.start()
+
+    slot = lax.broadcasted_iota(jnp.int32, (1, slots), 1)
+    key_r = jnp.where(slot < used, trow_v[...].reshape(1, slots), -1)
+    key_c = jnp.where(slot < used, tcol_v[...].reshape(1, slots), -1)
+    key_c = jnp.where(core == 0, key_c[:, :half], key_c[:, half:])
+    chosen_c[...] = (lax.broadcasted_iota(jnp.int32, (tiles_all, half), 0) == key_c).astype(F32).astype(BF)
     chosen_r[...] = (lax.broadcasted_iota(jnp.int32, (tiles_dev, slots), 0) == key_r).astype(F32).astype(BF)
 
     own_c.wait()
@@ -149,122 +180,181 @@
     to_col(3, lambda d: bstage.at[d], bgath.at[me_c])
     own_b = pltpu.make_async_copy(bstage.at[me_c], bgath.at[me_c], own_sem.at[3])
     own_b.start()
-    zero = jnp.zeros((16, TILE), BF)
-
-    def tile_pass(source, index_s, forward):
+
+    def tile_pass(sources, index_s, first, size, forward):
         group = 4 * unroll
+        count = len(sources)
+        depth = 16 * count
+        zero = jnp.zeros((depth, TILE), BF)
 
         def step(g, carry):
             for u in range(unroll):
                 s = pl.multiple_of(g * group, group) + 4 * u
-                at = [index_s[s + i] for i in range(4)]
-                x = [source[at[i] // 2] for i in range(4)]
+                at = [index_s[first + s + i] for i in range(4)]
+                x = [jnp.concatenate([ref[at[i] // 2] for ref in sources], axis=0) for i in range(4)]
                 spread = (
                     [[x[0], zero], [x[1], zero], [zero, x[2]], [zero, x[3]]]
                     if forward
                     else [[x[0], zero], [zero, x[1]], [x[2], zero], [zero, x[3]]]
                 )
                 left = jnp.concatenate([jnp.concatenate(pair, axis=1) for pair in spread], axis=0)
-                right = jnp.concatenate(
-                    [adj[pl.ds(s, 2)].reshape(2 * TILE, TILE), adj[pl.ds(s + 2, 2)].reshape(2 * TILE, TILE)], axis=1
-                )
+                tiles = [adj[pl.ds(first + s + 2 * i, 2)].reshape(2 * TILE, TILE) for i in range(2)]
+                right = jnp.concatenate(tiles, axis=1)
                 out = lax.dot_general(left, right, NT if forward else NN, preferred_element_type=F32)
                 for i in range(4):
-                    half = i % 2 if forward else i // 2
-                    block = out[16 * i:16 * i + 16, TILE * half:TILE * half + TILE]
-                    block = jnp.where(at[i] % 2 == 0, block[:8], block[8:])
-                    block = jnp.where(s + i < used, block, 0.0)
-                    prod[pl.ds(pl.multiple_of((s + i) * 8, 8), 8), :] = block
+                    side = i % 2 if forward else i // 2
+                    for j in range(count):
+                        top = depth * i + 16 * j
+                        block = out[top:top + 16, TILE * side:TILE * side + TILE]
+                        block = jnp.where(at[i] % 2 == 0, block[:8], block[8:])
+                        block = jnp.where(first + s + i < used, block, 0.0)
+                        prod[pl.ds(pl.multiple_of((j * size + s + i) * 8, 8), 8), :] = block
             return carry
 
         return step
 
-    def add_up(chosen, tiles):
+    def add_up(chosen, which, size, take, pairs=range(4)):
         picks = chosen[...]
-        for f in range(0, 8, 2):
-            pair = jnp.concatenate([prod[pl.ds(f + j, slots, stride=8), :] for j in range(2)], axis=1)
+        for f in [2 * p for p in pairs]:
+            top = which * size * 8 + f
+            pair = jnp.concatenate([prod[pl.ds(top + j, size, stride=8), :] for j in range(2)], axis=1)
             high = pair.astype(BF)
             low = (pair - high.astype(F32)).astype(BF)
             total = lax.dot_general(picks, high, NN, preferred_element_type=F32) + lax.dot_general(
                 picks, low, NN, preferred_element_type=F32
             )
             for j in range(2):
-                sums[pl.ds(f + j, tiles, stride=8), :] = total[:, TILE * j:TILE * j + TILE]
+                take(f + j, total[:, TILE * j:TILE * j + TILE])
 
     own_f.wait()
     arrived(2, fgath.at[pl.ds(0, rows - 1)])
-    features = fgath.reshape(rows * cols, 16, TILE)
     groups = slots // (4 * unroll)
-    forward = tile_pass(features, tcol_s, True)
+    late = groups - 2
+    forward = tile_pass([fgath.reshape(rows * cols, 16, TILE)], tcol_s, 0, slots, True)
 
     def forward_step(g, carry):
         adj_copy(g).wait()
         return forward(g, carry)
 
-    lax.fori_loop(0, groups, forward_step, 0)
-    add_up(chosen_r, tiles_dev)
+    lax.fori_loop(0, late, forward_step, 0)
+    own_b.wait()
+    arrived(3, bgath.at[pl.ds(0, cols - 1)])
+    to_pair(1, bgath, bsib)
+    own_l.wait()
+    arrived(8, cline.at[pl.ds(0, 3), 0])
+    to_pair(0, cline.at[:, core], cline.at[:, core])
+    lax.fori_loop(late, groups, forward_step, 0)
+
+    def take_pown(f, block):
+        pown[pl.ds(f * tiles_dev, tiles_dev), :] = block
+
+    add_up(chosen_r, 0, slots, take_pown)
     for d in range(cols):
         halves = []
         for h in range(2):
-            at = 2 * d + h
-            block = sums[8 * at:8 * at + 8, :]
-            halves.append(jnp.where(lane + at * TILE < live_count, block, 0.0))
+            t = 2 * d + h
+            block = pown[pl.ds(t, 8, stride=tiles_dev), :]
+            halves.append(jnp.where(lane + t * TILE < live_count, block, 0.0))
         astage[d] = jnp.concatenate(halves, axis=0).astype(BF)
     to_col(5, lambda d: astage.at[d], agath.at[me_c])
+    pltpu.make_async_remote_copy(
+        src_ref=astage, dst_ref=apart, send_sem=send_sem.at[6], recv_sem=recv_sem.at[6],
+        device_id=(me_r, partner), device_id_type=MESH,
+    ).start()
     own_a = pltpu.make_async_copy(astage.at[me_c], agath.at[me_c], own_sem.at[5])
     own_a.start()
-    own_b.wait()
-    arrived(3, bgath.at[pl.ds(0, cols - 1)])
-
-    backward = tile_pass(bgath, trow_s, False)
-    lax.fori_loop(0, groups - 1, backward, 0)
+
+    pair_arrived(1, bsib)
+    backward = tile_pass([bgath, bsib], trow_s, base, half, False)
+    lax.fori_loop(0, half // (4 * unroll), backward, 0)
+
+    def take_gsib(f, block):
+        gsib[f] = block.astype(BF)
+        if f % 2 == 1:
+            part = pl.ds(f - 1, 2)
+            to_pair(2 + f // 2, gsib.at[part], grecv.at[part])
+
+    def take_gown(f, block):
+        if f % 2 == 0:
+            pair_arrived(2 + f // 2, grecv.at[pl.ds(f, 2)])
+        block = (block + grecv[f].astype(F32)).astype(BF)
+        for d in range(rows):
+            gstage[d, f] = block[d * tiles_dev:(d + 1) * tiles_dev]
+
+    def to_owners(part):
+        here = pl.ds(4 * part, 4)
+
+        def one(k, carry):
+            peer = lax.rem(me_r + k, rows)
+            pltpu.make_async_remote_copy(
+                src_ref=gstage.at[peer, here], dst_ref=ggath.at[me_r, here],
+                send_sem=send_sem.at[9], recv_sem=grad_sem.at[part, me_r],
+                device_id=(peer, me_c), device_id_type=MESH,
+            ).start()
+            return carry
+
+        lax.fori_loop(1, rows, one, 0)
+
+    add_up(chosen_c, 1, half, take_gsib, (0, 1, 2))
+    pair_arrived(0, cline.at[:, 0])
+    arrived(6, astage)
+    both = []
+    for d in range(cols):
+        mine, theirs = astage[d].astype(F32), apart[d].astype(F32)
+        for h in range(2):
+            both.append(jnp.concatenate([mine[8 * h:8 * h + 8], theirs[8 * h:8 * h + 8]], axis=0).astype(BF))
+    left = jnp.concatenate(both, axis=1)
+    gw = lax.dot_general(left, cline[...].reshape(cols // 2 * 16, left.shape[1]), NT, preferred_element_type=F32)
+    wpart[...] = gw.reshape(2, 8, gw.shape[1])
+    wfinal[me_r, side_x] = gw[:8]
+    to_row(4, lambda d: wpart.at[0], wfinal.at[me_r, side_x])
+
+    def to_partner(k, carry):
+        pltpu.make_async_remote_copy(
+            src_ref=wpart.at[1], dst_ref=wfinal.at[me_r, side_x], send_sem=send_sem.at[4], recv_sem=recv_sem.at[4],
+            device_id=(lax.rem(me_r + k, rows), partner), device_id_type=MESH,
+        ).start()
+        return carry
+
+    lax.fori_loop(0, rows, to_partner, 0)
+
+    add_up(chosen_c, 0, half, take_gown, (0, 1))
+    to_owners(0)
+    add_up(chosen_c, 1, half, take_gsib, (3,))
+    add_up(chosen_c, 0, half, take_gown, (2, 3))
+    to_owners(1)
+
     own_a.wait()
     arrived(5, agath.at[pl.ds(0, cols - 1)])
-
     agg = unstack(agath)
-    gw = lax.dot_general(agg, cgath[...].reshape(cols * 16, 2 * TILE), NT, preferred_element_type=F32)
-    wpart[...] = gw.reshape(cols, 8, gw.shape[1])
-    to_col(6, lambda d: wpart.at[d], wpgath.at[me_c])
     whole_w = unstack(wgath)
     hidden = lax.dot_general(whole_w, agg, (((0,), (0,)), ((), ())), preferred_element_type=F32)
     hstage[...] = hidden.astype(BF).reshape(cols, 16, 2 * TILE)
     to_col(7, lambda d: hstage.at[d], hid_ref.at[:, slice_cols(me_c)])
     own_h = pltpu.make_async_copy(hstage.at[me_c], hid_ref.at[:, slice_cols(me_c)], own_sem.at[6])
     own_h.start()
-    own_p = pltpu.make_async_copy(wpart.at[me_c], wpgath.at[me_c], own_sem.at[7])
-    own_p.start()
-
-    lax.fori_loop(groups - 1, groups, backward, 0)
-    add_up(chosen_c, rows * tiles_dev)
-    for d in range(rows):
-        size = tiles_dev * 8
-        gstage[d] = sums[d * size:(d + 1) * size, :].reshape(cols, 16, TILE).astype(BF)
-    to_row(4, lambda d: gstage.at[d], ggath.at[me_r])
-    own_g = pltpu.make_async_copy(gstage.at[me_r], ggath.at[me_r], own_sem.at[4])
-    own_g.start()
-
-    own_p.wait()
-    arrived(6, wpgath.at[pl.ds(0, cols - 1)])
-    wrow[...] = jnp.sum(wpgath[...], axis=0)
-    to_row(8, lambda d: wrow, wrgath.at[me_r])
-    own_r = pltpu.make_async_copy(wrow, wrgath.at[me_r], own_sem.at[8])
-    own_r.start()
-    own_g.wait()
-    arrived(4, ggath.at[pl.ds(0, rows - 1)])
-    for p in range(cols):
-        total = ggath[0, p].astype(F32)
-        for d in range(1, rows):
-            total = total + ggath[d, p].astype(F32)
-        for h in range(2):
-            at = (2 * p + h) * TILE
-            gf_ref[:, at:at + TILE] = jnp.where(lane + at < live_count, total[8 * h:8 * h + 8], 0.0).astype(BF)
-
-    own_r.wait()
-    arrived(8, wrgath.at[pl.ds(0, rows - 1)])
-    total = wrgath[0]
+
+    arrived(4, wfinal.reshape(2 * rows, 8, wfinal.shape[3]).at[pl.ds(0, 2 * rows - 1)])
+    total = wfinal[0]
     for d in range(1, rows):
-        total = total + wrgath[d]
-    gw_ref[...] = total * float(node_total) ** (-0.5)
+        total = total + wfinal[d]
+    width = gw.shape[1] // 4
+    parts = [total[x, :, y * width:(y + 1) * width] for y in range(4) for x in range(2)]
+    gw_ref[...] = jnp.concatenate(parts, axis=1) * float(node_total) ** (-0.5)
+
+    x_me, z_me = me_r // (rows // 2), lax.rem(me_r, rows // 2)
+    for part in range(2):
+        here = pl.ds(4 * part, 4)
+        total = gstage[me_r, here].astype(F32)
+        for dx, dz in ((0, 1), (0, 3), (1, 0), (0, 2), (1, 1), (1, 3), (1, 2)):
+            source = lax.rem(x_me + dx, 2) * (rows // 2) + lax.rem(z_me + dz, rows // 2)
+            block = ggath.at[source, here]
+            pltpu.make_async_copy(block, block, grad_sem.at[part, source]).wait()
+            total = total + block[...].astype(F32)
+        gsum[pl.ds(4 * part * tiles_dev, 4 * tiles_dev), :] = total.reshape(4 * tiles_dev, TILE)
+    for t in range(tiles_dev):
+        block = gsum[pl.ds(t, 8, stride=tiles_dev), :]
+        gf_ref[:, t * TILE:(t + 1) * TILE] = jnp.where(lane + t * TILE < live_count, block, 0.0).astype(BF)
 
     own_h.wait()
     arrived(7, hstage.at[pl.ds(0, cols - 1)])
@@ -272,11 +362,16 @@
     sent(1, wgath.at[pl.ds(0, cols - 1)])
     sent(2, fgath.at[pl.ds(0, rows - 1)])
     sent(3, bgath.at[pl.ds(0, cols - 1)])
-    sent(4, ggath.at[pl.ds(0, rows - 1)])
+    sent(4, wfinal.reshape(2 * rows, 8, wfinal.shape[3]).at[pl.ds(0, 2 * rows - 1)])
     sent(5, agath.at[pl.ds(0, cols - 1)])
-    sent(6, wpgath.at[pl.ds(0, cols - 1)])
+    sent(6, astage)
     sent(7, hstage.at[pl.ds(0, cols - 1)])
-    sent(8, wrgath.at[pl.ds(0, rows - 1)])
+    sent(8, cline.at[pl.ds(0, 3), 0])
+    sent(9, ggath.at[pl.ds(0, rows - 1)])
+    pair_sent(0, cline.at[:, 0])
+    pair_sent(1, bsib)
+    for i in range(4):
+        pair_sent(2 + i, gsib.at[pl.ds(2 * i, 2)])
 
 
 def finish(a_in, b_in, c_in, a_out, b_out, c_out):
@@ -294,6 +389,7 @@
         hid = weight.shape[1]
         tiles = nodes // TILE
         unroll = 20
+        half = slots // 2
         groups = slots // (4 * unroll)
         smem = pl.BlockSpec(memory_space=pltpu.SMEM)
         vmem = pl.BlockSpec(memory_space=pltpu.VMEM)
@@ -319,24 +415,31 @@
                 pltpu.VMEM((cols, 16, hid // 2), BF),
                 pltpu.VMEM((cols, 16, TILE), BF),
                 pltpu.VMEM((cols, 16, TILE), BF),
+                pltpu.VMEM((cols, 16, TILE), BF),
+                pltpu.VMEM((4, 2) + cotangent.shape, BF),
                 pltpu.VMEM((slots * 8, TILE), F32),
-                pltpu.VMEM((rows * tiles * 8, TILE), F32),
-                pltpu.VMEM((rows, cols, 16, TILE), BF),
-                pltpu.VMEM((rows, cols, 16, TILE), BF),
+                pltpu.VMEM((8 * tiles, TILE), F32),
+                pltpu.VMEM((8, rows * tiles, TILE), BF),
+                pltpu.VMEM((8, rows * tiles, TILE), BF),
+                pltpu.VMEM((rows, 8, tiles, TILE), BF),
+                pltpu.VMEM((rows, 8, tiles, TILE), BF),
+                pltpu.VMEM((8 * tiles, TILE), F32),
+                pltpu.VMEM((cols, 16, TILE), BF),
                 pltpu.VMEM((cols, 16, TILE), BF),
                 pltpu.VMEM((cols, 16, TILE), BF),
                 pltpu.VMEM((cols, 16, 2 * TILE), BF),
-                pltpu.VMEM((cols, 8, hid), F32),
-                pltpu.VMEM((cols, 8, hid), F32),
-                pltpu.VMEM((8, hid), F32),
-                pltpu.VMEM((rows, 8, hid), F32),
-                pltpu.VMEM((rows * tiles, slots), BF),
+                pltpu.VMEM((2, 8, hid // 2), F32),
+                pltpu.VMEM((rows, 2, 8, hid // 2), F32),
+                pltpu.VMEM((rows * tiles, half), BF),
                 pltpu.VMEM((tiles, slots), BF),
                 pltpu.SemaphoreType.DMA((groups,)),
                 pltpu.SemaphoreType.DMA((3,)),
-                pltpu.SemaphoreType.DMA((9,)),
-                pltpu.SemaphoreType.DMA((9,)),
-                pltpu.SemaphoreType.DMA((9,)),
+                pltpu.SemaphoreType.DMA((8,)),
+                pltpu.SemaphoreType.DMA((10,)),
+                pltpu.SemaphoreType.DMA((10,)),
+                pltpu.SemaphoreType.DMA((6,)),
+                pltpu.SemaphoreType.DMA((6,)),
+                pltpu.SemaphoreType.DMA((2, rows)),
             ],
             compiler_params=pltpu.CompilerParams(
                 collective_id=0, has_side_effects=True, vmem_limit_bytes=60 * 2**20

time: 48.9 us -> 47.3 us (0.967)
  Pallas kernels: 46.7 us -> 45.2 us
    pallas_call x1, Pallas kernels: 45.1 us -> 43.6 us  [local(): pl.pallas_call(functools.partial(kernel, rows, cols, slots, groups, unrol...]
where the time goes in v4:
time: 47.3 us; the launch traced here: 47.1 us
  Pallas kernels  45.2 us (96%)
  between operations  1.93 us (4%)
    pallas_call x1, Pallas kernels, local(): pl.pallas_call(functools.partial(kernel, rows, cols, slots, groups, unrol...  43.6 us
    pallas_call x1, Pallas kernels, local(): pl.pallas_call(finish, out_shape=[jax.ShapeDtypeStruct(x.shape, x.dtype)...  1.61 us

profile of v4, /device:TPU:1, one launch (start us, length us, event | category | flops | bytes accessed | tf_op | source)
XLA Modules:
  0.0 47.1 jit_solution(8983281912548568057)
XLA Ops:
  1.9 43.6 %shard_map.103 = (bf16[16,4096]{1,0:T(8,128)(2,1)}, f32[8,256]{1,0:T(8,128)}, bf16[8,4096]{1,0:T(8,128)(2,1)}) custom-call(bf16[8,4096]{1,0:T(8,128)(2,1)} %feat_hbm.1, bf16[8,256]{1,0:T(8,128)(2,1)} %weight_hbm.1, bf16[16,4096]{1,0:T(8,128)(2,1)} %cot_hbm.1, bf16[640,128,128]{2,1,0:T(8,128)(2,1)} %adj_hbm.1, s32[640]{0:T(1024)} %trow_v.1, s32[640]{0:T(1024)} %tcol_v.1, ...), custom_call_target="tpu_custom_call" | custom-call | tf_op jit(solution)/shard_map/pallas_call | solution.py:397
  45.5 1.6 %shard_map.104 = (bf16[16,4096]{1,0:T(8,128)(2,1)}, f32[8,256]{1,0:T(8,128)}, bf16[8,4096]{1,0:T(8,128)(2,1)}) custom-call(bf16[16,4096]{1,0:T(8,128)(2,1)} %get-tuple-element.6.a_in, f32[8,256]{1,0:T(8,128)} %get-tuple-element.7.b_in, bf16[8,4096]{1,0:T(8,128)(2,1)} %get-tuple-element.8.c_in), custom_call_target="tpu_custom_call" | custom-call | tf_op jit(solution)/shard_map/pallas_call | solution.py:451

commit v5 on v4

--- a/solution.py
+++ b/solution.py
@@ -20,8 +20,8 @@
     feat_hbm, weight_hbm, cot_hbm, adj_hbm, trow_s, tcol_s, trow_v, tcol_v, tcount, ncount,
     hid_ref, gw_ref, gf_ref,
     feat_ref, weight_ref, cot_ref, adj, fstage, fgath, cgath, wstage, wgath, bstage, bgath, bsib, cline,
-    prod, pown, gsib, grecv, gstage, ggath, gsum,
-    astage, agath, apart, hstage, wpart, wfinal, chosen_c, chosen_r,
+    prod, pown, gsib, grecv, gstage, ggath, ends_v, ends,
+    astage, agath, apart, hstage, wpart, wfinal, chosen_r,
     adj_sem, in_sem, own_sem, send_sem, recv_sem, pair_send, pair_recv, grad_sem,
 ):
     me_r = lax.axis_index("row")
@@ -160,10 +160,19 @@
 
     slot = lax.broadcasted_iota(jnp.int32, (1, slots), 1)
     key_r = jnp.where(slot < used, trow_v[...].reshape(1, slots), -1)
-    key_c = jnp.where(slot < used, tcol_v[...].reshape(1, slots), -1)
+    key_c = jnp.where(slot < used, tcol_v[...].reshape(1, slots), tiles_all)
     key_c = jnp.where(core == 0, key_c[:, :half], key_c[:, half:])
-    chosen_c[...] = (lax.broadcasted_iota(jnp.int32, (tiles_all, half), 0) == key_c).astype(F32).astype(BF)
     chosen_r[...] = (lax.broadcasted_iota(jnp.int32, (tiles_dev, slots), 0) == key_r).astype(F32).astype(BF)
+
+    tile = lax.broadcasted_iota(jnp.int32, (tiles_all, half), 0)
+    upto = jnp.sum((key_c <= tile).astype(jnp.int32), axis=1, keepdims=True)
+    below = jnp.sum((key_c < tile).astype(jnp.int32), axis=1, keepdims=True)
+    last = jnp.broadcast_to(jnp.where(upto > below, upto - 1, slots), (tiles_all, TILE)).T[:8]
+    row = lax.broadcasted_iota(jnp.int32, last.shape, 0)
+    ends_v[...] = jnp.where((row == 1) & (last < slots), last + half, last)
+    table = pltpu.make_async_copy(ends_v, ends, in_sem.at[3])
+    table.start()
+    prod[slots] = jnp.zeros((8, TILE), F32)
 
     own_c.wait()
     own_w.wait()
@@ -180,6 +189,7 @@
     to_col(3, lambda d: bstage.at[d], bgath.at[me_c])
     own_b = pltpu.make_async_copy(bstage.at[me_c], bgath.at[me_c], own_sem.at[3])
     own_b.start()
+    table.wait()
 
     def tile_pass(sources, index_s, first, size, forward):
         group = 4 * unroll
@@ -187,7 +197,7 @@
         depth = 16 * count
         zero = jnp.zeros((depth, TILE), BF)
 
-        def step(g, carry):
+        def step(g, runs):
             for u in range(unroll):
                 s = pl.multiple_of(g * group, group) + 4 * u
                 at = [index_s[first + s + i] for i in range(4)]
@@ -208,16 +218,22 @@
                         block = out[top:top + 16, TILE * side:TILE * side + TILE]
                         block = jnp.where(at[i] % 2 == 0, block[:8], block[8:])
                         block = jnp.where(first + s + i < used, block, 0.0)
-                        prod[pl.ds(pl.multiple_of((j * size + s + i) * 8, 8), 8), :] = block
-            return carry
+                        if not forward:
+                            here = first + s + i
+                            same = tcol_s[here] == tcol_s[jnp.maximum(here - 1, 0)]
+                            block = block + jnp.where(same, runs[j], 0.0)
+                            runs = runs[:j] + (block,) + runs[j + 1:]
+                        prod[j * size + s + i] = block
+            return runs
 
         return step
 
     def add_up(chosen, which, size, take, pairs=range(4)):
         picks = chosen[...]
+        flat = prod.reshape((slots + 1) * 8, TILE)
         for f in [2 * p for p in pairs]:
             top = which * size * 8 + f
-            pair = jnp.concatenate([prod[pl.ds(top + j, size, stride=8), :] for j in range(2)], axis=1)
+            pair = jnp.concatenate([flat[pl.ds(top + j, size, stride=8), :] for j in range(2)], axis=1)
             high = pair.astype(BF)
             low = (pair - high.astype(F32)).astype(BF)
             total = lax.dot_general(picks, high, NN, preferred_element_type=F32) + lax.dot_general(
@@ -266,36 +282,23 @@
 
     pair_arrived(1, bsib)
     backward = tile_pass([bgath, bsib], trow_s, base, half, False)
-    lax.fori_loop(0, half // (4 * unroll), backward, 0)
-
-    def take_gsib(f, block):
-        gsib[f] = block.astype(BF)
-        if f % 2 == 1:
-            part = pl.ds(f - 1, 2)
-            to_pair(2 + f // 2, gsib.at[part], grecv.at[part])
-
-    def take_gown(f, block):
-        if f % 2 == 0:
-            pair_arrived(2 + f // 2, grecv.at[pl.ds(f, 2)])
-        block = (block + grecv[f].astype(F32)).astype(BF)
-        for d in range(rows):
-            gstage[d, f] = block[d * tiles_dev:(d + 1) * tiles_dev]
-
-    def to_owners(part):
-        here = pl.ds(4 * part, 4)
-
-        def one(k, carry):
-            peer = lax.rem(me_r + k, rows)
-            pltpu.make_async_remote_copy(
-                src_ref=gstage.at[peer, here], dst_ref=ggath.at[me_r, here],
-                send_sem=send_sem.at[9], recv_sem=grad_sem.at[part, me_r],
-                device_id=(peer, me_c), device_id_type=MESH,
-            ).start()
-            return carry
-
-        lax.fori_loop(1, rows, one, 0)
-
-    add_up(chosen_c, 1, half, take_gsib, (0, 1, 2))
+    lax.fori_loop(0, half // (4 * unroll), backward, (jnp.zeros((8, TILE), F32),) * 2)
+
+    def gathered(which, d, p):
+        t = d * tiles_dev + 2 * p
+        return jnp.concatenate([prod[ends[which, t]], prod[ends[which, t + 1]]], axis=0)
+
+    def to_sibling(k, carry):
+        d = lax.rem(me_r + k, rows)
+        for p in range(cols):
+            gsib[d, p] = gathered(1, d, p).astype(BF)
+        pltpu.make_async_remote_copy(
+            src_ref=gsib.at[d], dst_ref=grecv.at[d], send_sem=pair_send.at[2], recv_sem=pair_recv.at[2 + d],
+            device_id=(me_r, sibling), device_id_type=MESH,
+        ).start()
+        return carry
+
+    lax.fori_loop(1, rows + 1, to_sibling, 0)
     pair_arrived(0, cline.at[:, 0])
     arrived(6, astage)
     both = []
@@ -318,11 +321,22 @@
 
     lax.fori_loop(0, rows, to_partner, 0)
 
-    add_up(chosen_c, 0, half, take_gown, (0, 1))
-    to_owners(0)
-    add_up(chosen_c, 1, half, take_gsib, (3,))
-    add_up(chosen_c, 0, half, take_gown, (2, 3))
-    to_owners(1)
+    def own_share(d):
+        pair_arrived(2 + d, grecv.at[d])
+        for p in range(cols):
+            gstage[d, p] = (gathered(0, d, p) + grecv[d, p].astype(F32)).astype(BF)
+
+    def to_owner(k, carry):
+        d = lax.rem(me_r + k, rows)
+        own_share(d)
+        pltpu.make_async_remote_copy(
+            src_ref=gstage.at[d], dst_ref=ggath.at[me_r], send_sem=send_sem.at[9], recv_sem=grad_sem.at[me_r],
+            device_id=(d, me_c), device_id_type=MESH,
+        ).start()
+        return carry
+
+    lax.fori_loop(1, rows, to_owner, 0)
+    own_share(me_r)
 
     own_a.wait()
     arrived(5, agath.at[pl.ds(0, cols - 1)])
@@ -343,18 +357,16 @@
     gw_ref[...] = jnp.concatenate(parts, axis=1) * float(node_total) ** (-0.5)
 
     x_me, z_me = me_r // (rows // 2), lax.rem(me_r, rows // 2)
-    for part in range(2):
-        here = pl.ds(4 * part, 4)
-        total = gstage[me_r, here].astype(F32)
-        for dx, dz in ((0, 1), (0, 3), (1, 0), (0, 2), (1, 1), (1, 3), (1, 2)):
-            source = lax.rem(x_me + dx, 2) * (rows // 2) + lax.rem(z_me + dz, rows // 2)
-            block = ggath.at[source, here]
-            pltpu.make_async_copy(block, block, grad_sem.at[part, source]).wait()
-            total = total + block[...].astype(F32)
-        gsum[pl.ds(4 * part * tiles_dev, 4 * tiles_dev), :] = total.reshape(4 * tiles_dev, TILE)
-    for t in range(tiles_dev):
-        block = gsum[pl.ds(t, 8, stride=tiles_dev), :]
-        gf_ref[:, t * TILE:(t + 1) * TILE] = jnp.where(lane + t * TILE < live_count, block, 0.0).astype(BF)
+    total = gstage[me_r].astype(F32)
+    for dx, dz in ((0, 1), (0, 3), (1, 0), (0, 2), (1, 1), (1, 3), (1, 2)):
+        source = lax.rem(x_me + dx, 2) * (rows // 2) + lax.rem(z_me + dz, rows // 2)
+        block = ggath.at[source]
+        pltpu.make_async_copy(block, block, grad_sem.at[source]).wait()
+        total = total + block[...].astype(F32)
+    for p in range(cols):
+        for h in range(2):
+            at = (2 * p + h) * TILE
+            gf_ref[:, at:at + TILE] = jnp.where(lane + at < live_count, total[p, 8 * h:8 * h + 8], 0.0).astype(BF)
 
     own_h.wait()
     arrived(7, hstage.at[pl.ds(0, cols - 1)])
@@ -370,8 +382,7 @@
     sent(9, ggath.at[pl.ds(0, rows - 1)])
     pair_sent(0, cline.at[:, 0])
     pair_sent(1, bsib)
-    for i in range(4):
-        pair_sent(2 + i, gsib.at[pl.ds(2 * i, 2)])
+    pair_sent(2, gsib)
 
 
 def finish(a_in, b_in, c_in, a_out, b_out, c_out):
@@ -388,7 +399,7 @@
         feats, nodes = features.shape
         hid = weight.shape[1]
         tiles = nodes // TILE
-        unroll = 20
+        unroll = 40
         half = slots // 2
         groups = slots // (4 * unroll)
         smem = pl.BlockSpec(memory_space=pltpu.SMEM)
@@ -417,29 +428,29 @@
                 pltpu.VMEM((cols, 16, TILE), BF),
                 pltpu.VMEM((cols, 16, TILE), BF),
                 pltpu.VMEM((4, 2) + cotangent.shape, BF),
-                pltpu.VMEM((slots * 8, TILE), F32),
+                pltpu.VMEM((slots + 1, 8, TILE), F32),
                 pltpu.VMEM((8 * tiles, TILE), F32),
-                pltpu.VMEM((8, rows * tiles, TILE), BF),
-                pltpu.VMEM((8, rows * tiles, TILE), BF),
-                pltpu.VMEM((rows, 8, tiles, TILE), BF),
-                pltpu.VMEM((rows, 8, tiles, TILE), BF),
-                pltpu.VMEM((8 * tiles, TILE), F32),
+                pltpu.VMEM((rows, cols, 16, TILE), BF),
+                pltpu.VMEM((rows, cols, 16, TILE), BF),
+                pltpu.VMEM((rows, cols, 16, TILE), BF),
+                pltpu.VMEM((rows, cols, 16, TILE), BF),
+                pltpu.VMEM((8, rows * tiles), jnp.int32),
+                pltpu.SMEM((8, rows * tiles), jnp.int32),
                 pltpu.VMEM((cols, 16, TILE), BF),
                 pltpu.VMEM((cols, 16, TILE), BF),
                 pltpu.VMEM((cols, 16, TILE), BF),
                 pltpu.VMEM((cols, 16, 2 * TILE), BF),
                 pltpu.VMEM((2, 8, hid // 2), F32),
                 pltpu.VMEM((rows, 2, 8, hid // 2), F32),
-                pltpu.VMEM((rows * tiles, half), BF),
                 pltpu.VMEM((tiles, slots), BF),
                 pltpu.SemaphoreType.DMA((groups,)),
-                pltpu.SemaphoreType.DMA((3,)),
+                pltpu.SemaphoreType.DMA((4,)),
                 pltpu.SemaphoreType.DMA((8,)),
                 pltpu.SemaphoreType.DMA((10,)),
                 pltpu.SemaphoreType.DMA((10,)),
-                pltpu.SemaphoreType.DMA((6,)),
-                pltpu.SemaphoreType.DMA((6,)),
-                pltpu.SemaphoreType.DMA((2, rows)),
+                pltpu.SemaphoreType.DMA((3,)),
+                pltpu.SemaphoreType.DMA((2 + rows,)),
+                pltpu.SemaphoreType.DMA((rows,)),
             ],
             compiler_params=pltpu.CompilerParams(
                 collective_id=0, has_side_effects=True, vmem_limit_bytes=60 * 2**20

time: 47.3 us -> 47.4 us (level)
  no operation moved by 1% of the time
where the time goes in v5:
time: 47.4 us; the launch traced here: 47.2 us
  Pallas kernels  45.3 us (96%)
  between operations  1.93 us (4%)
    pallas_call x1, Pallas kernels, local(): pl.pallas_call(functools.partial(kernel, rows, cols, slots, groups, unrol...  43.7 us
    pallas_call x1, Pallas kernels, local(): pl.pallas_call(finish, out_shape=[jax.ShapeDtypeStruct(x.shape, x.dtype)...  1.61 us

profile of v5, /device:TPU:1, one launch (start us, length us, event | category | flops | bytes accessed | tf_op | source)
XLA Modules:
  0.0 47.2 jit_solution(982532322180295268)
XLA Ops:
  1.9 43.7 %shard_map.103 = (bf16[16,4096]{1,0:T(8,128)(2,1)}, f32[8,256]{1,0:T(8,128)}, bf16[8,4096]{1,0:T(8,128)(2,1)}) custom-call(bf16[8,4096]{1,0:T(8,128)(2,1)} %feat_hbm.1, bf16[8,256]{1,0:T(8,128)(2,1)} %weight_hbm.1, bf16[16,4096]{1,0:T(8,128)(2,1)} %cot_hbm.1, bf16[640,128,128]{2,1,0:T(8,128)(2,1)} %adj_hbm.1, s32[640]{0:T(1024)} %trow_v.1, s32[640]{0:T(1024)} %tcol_v.1, ...), custom_call_target="tpu_custom_call" | custom-call | tf_op jit(solution)/shard_map/pallas_call | solution.py:408
  45.6 1.6 %shard_map.104 = (bf16[16,4096]{1,0:T(8,128)(2,1)}, f32[8,256]{1,0:T(8,128)}, bf16[8,4096]{1,0:T(8,128)(2,1)}) custom-call(bf16[16,4096]{1,0:T(8,128)(2,1)} %get-tuple-element.6.a_in, f32[8,256]{1,0:T(8,128)} %get-tuple-element.7.b_in, bf16[8,4096]{1,0:T(8,128)(2,1)} %get-tuple-element.8.c_in), custom_call_target="tpu_custom_call" | custom-call | tf_op jit(solution)/shard_map/pallas_call | solution.py:462
